TPU v7x, 512 devices: a whole 4x4x16 slice. The times are simulated.
512 devices in a mesh: gx: 32 (over x, z_hi, y), gy: 16 (over z_lo, core).
Axes of the slice: x: 4, y: 4, z: 16 (z_hi: 2, z_lo: 8; z = z_hi * 8 + z_lo), core: 2. Of those that a mesh axis runs over, the one named last changes fastest.
Arguments:
- start_vectors: bfloat16 [128, 32, 128, 128], P('gx', 'gy'), may hold values from -6 to 6
- blocks: bfloat16 [128, 32, 7, 128, 128], P('gx', 'gy'), as said below
- neighbour: int32 [128, 32, 7], P('gx', 'gy'), may hold values from 0 to 8, as said below
- counts: int32 [128, 32], P('gx', 'gy'), may hold values from 1 to 7, as said below
Outputs:
- moments: float32 [5, 128], replicated
- last_vector: bfloat16 [128, 32, 128, 128], P('gx', 'gy')
Inputs may be any that keep to these rules, and one draw needn't show every extreme that they name: `neighbour`: each tile's 7 slots name the codes 0, 1, 3, 4, 5, 7, 8 once each, its live slots first; code 4 (the tile itself) is always live; tile t couples to tile t + d through a live slot exactly when tile t + d couples to t through a live slot of the opposite code. `counts`: one plus the number of the tile's live couplings to other tiles. The block of a live coupling of tile t + d back to tile t is the transpose of the block of tile t towards t + d; blocks of code 4 are symmetric.
All inputs are finite; a program needn't handle non-finite values.
Results may differ from a plain program's by a relative error of at most 0.0045.
Values may be sent and summed in bfloat16 or wider, within the bound.
A program may use at most 64 MiB of HBM per device.

v0:
```python
import jax
import jax.numpy as jnp
from jax import lax
from jax.sharding import PartitionSpec as P

ITERS = 4


def with_halo(cells, sides, width):
    for axis, dim in sides:
        count = lax.axis_size(axis)
        head = lax.slice_in_dim(cells, 0, width, axis=dim)
        tail = lax.slice_in_dim(cells, cells.shape[dim] - width, cells.shape[dim], axis=dim)
        cells = jnp.concatenate(
            [
                lax.ppermute(tail, axis, [(i, (i + 1) % count) for i in range(count)]),
                cells,
                lax.ppermute(head, axis, [((i + 1) % count, i) for i in range(count)]),
            ],
            axis=dim,
        )
    return cells


def local_apply(extended, blocks, neighbour, counts):
    tiles_x, tiles_y, slots = neighbour.shape
    vectors, orbitals = (extended.shape[2], extended.shape[3])
    flat = extended.reshape((tiles_x + 2) * (tiles_y + 2), vectors, orbitals)
    xs = jnp.arange(tiles_x, dtype=jnp.int32)[:, None] + 1
    ys = jnp.arange(tiles_y, dtype=jnp.int32)[None, :] + 1
    total = jnp.zeros((tiles_x, tiles_y, vectors, orbitals), jnp.float32)
    for slot in range(slots):
        code = neighbour[:, :, slot]
        index = (xs + code // 3 - 1) * (tiles_y + 2) + (ys + code % 3 - 1)
        piece = jnp.take(flat, index, axis=0)
        product = jnp.einsum(
            "xyrb,xyba->xyra", piece, blocks[:, :, slot], preferred_element_type=jnp.float32
        )
        live = (slot < counts).astype(jnp.float32)[:, :, None, None]
        total = total + live * product
    return total


def extend(vectors):
    along_x = with_halo(vectors, (("gx", 0),), 1)
    return with_halo(along_x, (("gy", 1),), 1)


def on_device(start_vectors, blocks, neighbour, counts):
    tiles_x, tiles_y = counts.shape
    total_rows = (
        tiles_x * lax.axis_size("gx") * tiles_y * lax.axis_size("gy") * start_vectors.shape[3]
    )
    first = start_vectors.astype(jnp.float32)
    partials = [jnp.sum(first * first, axis=(0, 1, 3))]
    previous = first
    current = local_apply(extend(start_vectors), blocks, neighbour, counts)
    partials.append(jnp.sum(first * current, axis=(0, 1, 3)))
    for step in range(ITERS - 1):
        image = local_apply(extend(current.astype(jnp.bfloat16)), blocks, neighbour, counts)
        following = 2.0 * image - previous
        previous, current = (current, following)
        partials.append(jnp.sum(first * current, axis=(0, 1, 3)))
    summed = jnp.stack([lax.psum(term, ("gx", "gy")) for term in partials])
    return (summed / total_rows, current.astype(jnp.bfloat16))


def solution(mesh):
    in_specs = (
        P("gx", "gy", None, None),
        P("gx", "gy", None, None, None),
        P("gx", "gy", None),
        P("gx", "gy"),
    )
    out_specs = (P(), P("gx", "gy", None, None))
    return jax.shard_map(
        on_device, mesh=mesh, in_specs=in_specs, out_specs=out_specs, check_vma=False
    )
```

profile of v0, /device:TPU:1, one launch (start us, length us, event | category | flops | bytes accessed | tf_op | source)
XLA Modules:
  0.0 365.0 jit_solution(12642964493823538940)
XLA Ops:
  1.5 4.0 %collective-permute-start = (bf16[1,2,128,128]{3,2,1,0:T(8,128)(2,1)S(1)}, bf16[1,2,128,128]{3,2,1,0:T(8,128)(2,1)S(1)}, u32[]{:S(2)}, u32[]{:S(2)}) collective-permute-start(bf16[1,2,128,128]{3,2,1,0:T(8,128)(2,1)S(1)} %get-tuple-element.49), channel_id=1, source_target_pairs={{0,16},{16,32},{32,48},{48,64},{64,80},{80,96},{96,112},{112,128},... | collective-permute-start | bytes 196616 | tf_op jit(solution)/shard_map/ppermute | solution.py:16
  5.6 18.8 %collective-permute-start.1 = (bf16[1,2,128,128]{3,2,1,0:T(8,128)(2,1)S(1)}, bf16[1,2,128,128]{3,2,1,0:T(8,128)(2,1)S(1)}, u32[]{:S(2)}, u32[]{:S(2)}) collective-permute-start(bf16[1,2,128,128]{3,2,1,0:T(8,128)(2,1)S(1)} %get-tuple-element.48), channel_id=1, source_target_pairs={{16,0},{32,16},{48,32},{64,48},{80,64},{96,80},{112,96},{128,112},... | collective-permute-start | bytes 196616 | tf_op jit(solution)/shard_map/ppermute | solution.py:18
  32.2 4.7 %collective-permute-start.3 = (bf16[6,1,128,128]{3,2,1,0:T(8,128)(2,1)S(1)}, bf16[6,1,128,128]{3,2,1,0:T(8,128)(2,1)S(1)}, u32[]{:S(2)}, u32[]{:S(2)}) collective-permute-start(bf16[6,1,128,128]{3,2,1,0:T(8,128)(2,1)S(1)} %get-tuple-element.41), channel_id=1, source_target_pairs={{1,0},{2,1},{3,2},{4,3},{5,4},{6,5},{7,6},{8,7},{9,8},{10,9},{11,1... | collective-permute-start | bytes 589832 | tf_op jit(solution)/shard_map/ppermute | solution.py:18
  36.9 1.9 collective-permute-start.2
  39.2 5.3 %collective-permute-done.2 = bf16[6,1,128,128]{3,2,1,0:T(8,128)(2,1)S(1)} collective-permute-done((bf16[6,1,128,128]{3,2,1,0:T(8,128)(2,1)S(1)}, bf16[6,1,128,128]{3,2,1,0:T(8,128)(2,1)S(1)}, u32[]{:S(2)}, u32[]{:S(2)}) %collective-permute-start.2) | collective-permute-done | bytes 196640 | tf_op jit(solution)/shard_map/ppermute | solution.py:16
  56.4 12.2 %collective-permute-start.5 = (bf16[1,2,128,128]{2,3,1,0:T(8,128)(2,1)S(1)}, bf16[1,2,128,128]{2,3,1,0:T(8,128)(2,1)S(1)}, u32[]{:S(2)}, u32[]{:S(2)}) collective-permute-start(bf16[1,2,128,128]{2,3,1,0:T(8,128)(2,1)S(1)} %get-tuple-element.47), channel_id=1, source_target_pairs={{16,0},{32,16},{48,32},{64,48},{80,64},{96,80},{112,96},{128,112},... | collective-permute-start | bytes 196616 | tf_op jit(solution)/shard_map/ppermute | solution.py:18
  68.6 1.9 collective-permute-start.4
  70.5 2.8 collective-permute-done.5
  73.3 13.4 %collective-permute-done.4 = bf16[1,2,128,128]{2,3,1,0:T(8,128)(2,1)S(1)} collective-permute-done((bf16[1,2,128,128]{2,3,1,0:T(8,128)(2,1)S(1)}, bf16[1,2,128,128]{2,3,1,0:T(8,128)(2,1)S(1)}, u32[]{:S(2)}, u32[]{:S(2)}) %collective-permute-start.4) | collective-permute-done | bytes 65568 | tf_op jit(solution)/shard_map/ppermute | solution.py:16
  87.4 12.2 %collective-permute-start.7 = (bf16[6,1,128,128]{2,3,1,0:T(8,128)(2,1)}, bf16[6,1,128,128]{2,3,1,0:T(8,128)(2,1)S(1)}, u32[]{:S(2)}, u32[]{:S(2)}) collective-permute-start(bf16[6,1,128,128]{2,3,1,0:T(8,128)(2,1)} %get-tuple-element.39), channel_id=1, source_target_pairs={{1,0},{2,1},{3,2},{4,3},{5,4},{6,5},{7,6},{8,7},{9,8},{10,9},{11,1... | collective-permute-start | bytes 589832 | tf_op jit(solution)/shard_map/ppermute | solution.py:18
  99.6 1.9 collective-permute-start.6
  103.1 1.6 collective-permute-done.6
  106.6 1.4 gather_fusion.8
  108.0 1.4 gather_fusion.9
  109.4 1.4 gather_fusion.10
  110.8 1.4 gather_fusion.11
  112.2 1.4 gather_fusion.12
  117.2 1.8 copy.264
  119.0 1.8 copy.265
  120.8 1.8 copy.266
  122.6 1.8 copy.267
  131.5 1.9 collective-permute-start.9
  133.5 3.4 collective-permute-start.8
  136.9 14.6 %collective-permute-done.8 = bf16[1,2,128,128]{2,3,1,0:T(8,128)(2,1)S(1)} collective-permute-done((bf16[1,2,128,128]{2,3,1,0:T(8,128)(2,1)S(1)}, bf16[1,2,128,128]{2,3,1,0:T(8,128)(2,1)S(1)}, u32[]{:S(2)}, u32[]{:S(2)}) %collective-permute-start.8) | collective-permute-done | bytes 65568 | tf_op jit(solution)/shard_map/ppermute | solution.py:16
  151.6 11.8 %collective-permute-start.11 = (bf16[6,1,128,128]{2,3,1,0:T(8,128)(2,1)S(1)}, bf16[6,1,128,128]{2,3,1,0:T(8,128)(2,1)S(1)}, u32[]{:S(2)}, u32[]{:S(2)}) collective-permute-start(bf16[6,1,128,128]{2,3,1,0:T(8,128)(2,1)S(1)} %get-tuple-element.37), channel_id=1, source_target_pairs={{1,0},{2,1},{3,2},{4,3},{5,4},{6,5},{7,6},{8,7},{9,8},{10,9},{11,1... | collective-permute-start | bytes 589832 | tf_op jit(solution)/shard_map/ppermute | solution.py:18
  163.3 1.9 collective-permute-start.10
  165.3 2.9 collective-permute-done.10
  177.3 1.8 copy.270
  180.5 1.8 copy.271
  182.3 1.8 copy.272
  184.1 1.8 copy.273
  185.9 1.8 copy.274
  189.7 1.4 fusion.15
  191.1 1.4 fusion.14
  195.0 1.9 collective-permute-start.13
  196.9 3.4 collective-permute-start.12
  200.3 14.7 %collective-permute-done.12 = bf16[1,2,128,128]{2,3,1,0:T(8,128)(2,1)S(1)} collective-permute-done((bf16[1,2,128,128]{2,3,1,0:T(8,128)(2,1)S(1)}, bf16[1,2,128,128]{2,3,1,0:T(8,128)(2,1)S(1)}, u32[]{:S(2)}, u32[]{:S(2)}) %collective-permute-start.12) | collective-permute-done | bytes 65568 | tf_op jit(solution)/shard_map/ppermute | solution.py:16
  215.1 11.8 %collective-permute-start.15 = (bf16[6,1,128,128]{2,3,1,0:T(8,128)(2,1)S(1)}, bf16[6,1,128,128]{2,3,1,0:T(8,128)(2,1)S(1)}, u32[]{:S(2)}, u32[]{:S(2)}) collective-permute-start(bf16[6,1,128,128]{2,3,1,0:T(8,128)(2,1)S(1)} %get-tuple-element.35), channel_id=1, source_target_pairs={{1,0},{2,1},{3,2},{4,3},{5,4},{6,5},{7,6},{8,7},{9,8},{10,9},{11,1... | collective-permute-start | bytes 589832 | tf_op jit(solution)/shard_map/ppermute | solution.py:18
  226.9 2.1 collective-permute-start.14
  229.0 2.8 collective-permute-done.14
  240.9 1.8 copy.277
  244.1 1.8 copy.278
  246.7 1.8 copy.280
  248.5 1.8 copy.281
  250.3 1.8 copy.282
  253.2 1.4 fusion.7
  254.6 1.4 fusion.6
  258.1 105.4 %all-reduce = (f32[1,128]{1,0:T(1,128)S(1)}, f32[1,128]{1,0:T(1,128)S(1)}, f32[1,128]{1,0:T(1,128)S(1)}, f32[1,128]{1,0:T(1,128)S(1)}, f32[1,128]{1,0:T(1,128)S(1)}) all-reduce(f32[1,128]{1,0:T(1,128)S(1)} %bitcast.259, f32[1,128]{1,0:T(1,128)S(1)} %bitcast.256, ...), channel_id=1, replica_groups=mesh['gx'=32,'gy'=16] {'gx','gy'}, use_global_device_ids=true, to_apply=%region_1.2 | all-reduce | flops 640 | bytes 5120 | tf_op jit(solution)/shard_map/psum | solution.py:64
  (261 shorter events, 66.3 us)
Async XLA Ops:
  1.5 29.6 %collective-permute-start = (bf16[1,2,128,128]{3,2,1,0:T(8,128)(2,1)S(1)}, bf16[1,2,128,128]{3,2,1,0:T(8,128)(2,1)S(1)}, u32[]{:S(2)}, u32[]{:S(2)}) collective-permute-start(bf16[1,2,128,128]{3,2,1,0:T(8,128)(2,1)S(1)} %get-tuple-element.49), channel_id=1, source_target_pairs={{0,16},{16,32},{32,48},{48,64},{64,80},{80,96},{96,112},{112,128},... | collective-permute-start | bytes 196616 | tf_op jit(solution)/shard_map/ppermute | solution.py:16
  5.6 26.5 %collective-permute-start.1 = (bf16[1,2,128,128]{3,2,1,0:T(8,128)(2,1)S(1)}, bf16[1,2,128,128]{3,2,1,0:T(8,128)(2,1)S(1)}, u32[]{:S(2)}, u32[]{:S(2)}) collective-permute-start(bf16[1,2,128,128]{3,2,1,0:T(8,128)(2,1)S(1)} %get-tuple-element.48), channel_id=1, source_target_pairs={{16,0},{32,16},{48,32},{64,48},{80,64},{96,80},{112,96},{128,112},... | collective-permute-start | bytes 196616 | tf_op jit(solution)/shard_map/ppermute | solution.py:18
  28.4 23.2 %copy-start.52 = (pred[4,2]{1,0:T(4,128)(4,1)}, pred[4,2]{1,0:T(4,128)(4,1)S(1)}, u32[]{:S(2)}) copy-start(pred[4,2]{1,0:T(4,128)(4,1)S(1)} %get-tuple-element.74) | copy-start | bytes 28
  28.4 27.2 %copy-start.50 = (pred[4,2]{1,0:T(4,128)(4,1)}, pred[4,2]{1,0:T(4,128)(4,1)S(1)}, u32[]{:S(2)}) copy-start(pred[4,2]{1,0:T(4,128)(4,1)S(1)} %get-tuple-element.21) | copy-start | bytes 28
  30.0 22.9 %copy-start.48 = (pred[4,2]{1,0:T(4,128)(4,1)}, pred[4,2]{1,0:T(4,128)(4,1)S(1)}, u32[]{:S(2)}) copy-start(pred[4,2]{1,0:T(4,128)(4,1)S(1)} %get-tuple-element.64) | copy-start | bytes 28
  30.0 24.3 %copy-start.46 = (pred[4,2]{1,0:T(4,128)(4,1)}, pred[4,2]{1,0:T(4,128)(4,1)S(1)}, u32[]{:S(2)}) copy-start(pred[4,2]{1,0:T(4,128)(4,1)S(1)} %get-tuple-element.66) | copy-start | bytes 28
  30.1 24.7 %copy-start.44 = (pred[4,2]{1,0:T(4,128)(4,1)}, pred[4,2]{1,0:T(4,128)(4,1)S(1)}, u32[]{:S(2)}) copy-start(pred[4,2]{1,0:T(4,128)(4,1)S(1)} %get-tuple-element.68) | copy-start | bytes 28
  30.1 25.1 %copy-start.42 = (pred[4,2]{1,0:T(4,128)(4,1)}, pred[4,2]{1,0:T(4,128)(4,1)S(1)}, u32[]{:S(2)}) copy-start(pred[4,2]{1,0:T(4,128)(4,1)S(1)} %get-tuple-element.70) | copy-start | bytes 28
  30.1 25.9 %copy-start.54 = (pred[4,2]{1,0:T(4,128)(4,1)}, pred[4,2]{1,0:T(4,128)(4,1)S(1)}, u32[]{:S(2)}) copy-start(pred[4,2]{1,0:T(4,128)(4,1)S(1)} %get-tuple-element.19) | copy-start | bytes 28
  30.9 25.0 %copy-start.26 = (f32[4,2]{1,0:T(4,128)}, f32[4,2]{1,0:T(4,128)S(1)}, u32[]{:S(2)}) copy-start(f32[4,2]{1,0:T(4,128)S(1)} %copy.253) | copy-start | bytes 100
  31.0 14.9 %copy-start.30 = (s32[1024]{0:T(1024)}, s32[1024]{0:T(1024)S(1)}, u32[]{:S(2)}) copy-start(s32[1024]{0:T(1024)S(1)} %get-tuple-element.100) | copy-start | bytes 12292
  31.0 16.2 %copy-start.28 = (s32[1024]{0:T(1024)}, s32[1024]{0:T(1024)S(1)}, u32[]{:S(2)}) copy-start(s32[1024]{0:T(1024)S(1)} %get-tuple-element.99) | copy-start | bytes 12292
  31.0 17.5 %copy-start.34 = (s32[1024]{0:T(1024)}, s32[1024]{0:T(1024)S(1)}, u32[]{:S(2)}) copy-start(s32[1024]{0:T(1024)S(1)} %get-tuple-element.98) | copy-start | bytes 12292
  31.0 18.7 %copy-start.32 = (s32[1024]{0:T(1024)}, s32[1024]{0:T(1024)S(1)}, u32[]{:S(2)}) copy-start(s32[1024]{0:T(1024)S(1)} %get-tuple-element.97) | copy-start | bytes 12292
  31.0 19.3 %copy-start.38 = (s32[1024]{0:T(1024)}, s32[1024]{0:T(1024)S(1)}, u32[]{:S(2)}) copy-start(s32[1024]{0:T(1024)S(1)} %get-tuple-element.96) | copy-start | bytes 12292
  31.0 19.9 %copy-start.36 = (s32[1024]{0:T(1024)}, s32[1024]{0:T(1024)S(1)}, u32[]{:S(2)}) copy-start(s32[1024]{0:T(1024)S(1)} %get-tuple-element.95) | copy-start | bytes 12292
  31.1 14.8 %copy-start.40 = (s32[1024]{0:T(1024)}, s32[1024]{0:T(1024)S(1)}, u32[]{:S(2)}) copy-start(s32[1024]{0:T(1024)S(1)} %pad_clamp_fusion.6) | copy-start | bytes 12292
  32.2 7.1 %collective-permute-start.3 = (bf16[6,1,128,128]{3,2,1,0:T(8,128)(2,1)S(1)}, bf16[6,1,128,128]{3,2,1,0:T(8,128)(2,1)S(1)}, u32[]{:S(2)}, u32[]{:S(2)}) collective-permute-start(bf16[6,1,128,128]{3,2,1,0:T(8,128)(2,1)S(1)} %get-tuple-element.41), channel_id=1, source_target_pairs={{1,0},{2,1},{3,2},{4,3},{5,4},{6,5},{7,6},{8,7},{9,8},{10,9},{11,1... | collective-permute-start | bytes 589832 | tf_op jit(solution)/shard_map/ppermute | solution.py:18
  36.9 7.6 %collective-permute-start.2 = (bf16[6,1,128,128]{3,2,1,0:T(8,128)(2,1)S(1)}, bf16[6,1,128,128]{3,2,1,0:T(8,128)(2,1)S(1)}, u32[]{:S(2)}, u32[]{:S(2)}) collective-permute-start(bf16[6,1,128,128]{3,2,1,0:T(8,128)(2,1)S(1)} %get-tuple-element.40), channel_id=1, source_target_pairs={{0,1},{1,2},{2,3},{3,4},{4,5},{5,6},{6,7},{7,8},{8,9},{9,10},{10,1... | collective-permute-start | bytes 589832 | tf_op jit(solution)/shard_map/ppermute | solution.py:16
  38.8 12.7 %copy-start.24 = (f32[4,2]{1,0:T(4,128)}, f32[4,2]{1,0:T(4,128)S(1)}, u32[]{:S(2)}) copy-start(f32[4,2]{1,0:T(4,128)S(1)} %get-tuple-element.59) | copy-start | bytes 100
  38.8 15.9 %copy-start.22 = (f32[4,2]{1,0:T(4,128)}, f32[4,2]{1,0:T(4,128)S(1)}, u32[]{:S(2)}) copy-start(f32[4,2]{1,0:T(4,128)S(1)} %get-tuple-element.58) | copy-start | bytes 100
  44.6 7.0 %copy-start = (bf16[4,2,7,128,128]{4,3,2,1,0:T(8,128)(2,1)S(1)}, bf16[4,2,7,128,128]{4,3,2,1,0:T(8,128)(2,1)}, u32[]{:S(2)}) copy-start(bf16[4,2,7,128,128]{4,3,2,1,0:T(8,128)(2,1)} %param.7) | copy-start | bytes 5505028
  55.9 45.6 %copy-start.4 = (bf16[4,2,128,128]{3,2,1,0:T(8,128)(2,1)S(1)}, bf16[4,2,128,128]{3,2,1,0:T(8,128)(2,1)}, u32[]{:S(2)}) copy-start(bf16[4,2,128,128]{3,2,1,0:T(8,128)(2,1)} %param.6) | copy-start | bytes 786436
  56.4 16.9 %collective-permute-start.5 = (bf16[1,2,128,128]{2,3,1,0:T(8,128)(2,1)S(1)}, bf16[1,2,128,128]{2,3,1,0:T(8,128)(2,1)S(1)}, u32[]{:S(2)}, u32[]{:S(2)}) collective-permute-start(bf16[1,2,128,128]{2,3,1,0:T(8,128)(2,1)S(1)} %get-tuple-element.47), channel_id=1, source_target_pairs={{16,0},{32,16},{48,32},{64,48},{80,64},{96,80},{112,96},{128,112},... | collective-permute-start | bytes 196616 | tf_op jit(solution)/shard_map/ppermute | solution.py:18
  68.6 18.1 %collective-permute-start.4 = (bf16[1,2,128,128]{2,3,1,0:T(8,128)(2,1)S(1)}, bf16[1,2,128,128]{2,3,1,0:T(8,128)(2,1)S(1)}, u32[]{:S(2)}, u32[]{:S(2)}) collective-permute-start(bf16[1,2,128,128]{2,3,1,0:T(8,128)(2,1)S(1)} %get-tuple-element.46), channel_id=1, source_target_pairs={{0,16},{16,32},{32,48},{48,64},{64,80},{80,96},{96,112},{112,128},... | collective-permute-start | bytes 196616 | tf_op jit(solution)/shard_map/ppermute | solution.py:16
  87.4 15.0 %collective-permute-start.7 = (bf16[6,1,128,128]{2,3,1,0:T(8,128)(2,1)}, bf16[6,1,128,128]{2,3,1,0:T(8,128)(2,1)S(1)}, u32[]{:S(2)}, u32[]{:S(2)}) collective-permute-start(bf16[6,1,128,128]{2,3,1,0:T(8,128)(2,1)} %get-tuple-element.39), channel_id=1, source_target_pairs={{1,0},{2,1},{3,2},{4,3},{5,4},{6,5},{7,6},{8,7},{9,8},{10,9},{11,1... | collective-permute-start | bytes 589832 | tf_op jit(solution)/shard_map/ppermute | solution.py:18
  99.6 5.1 %collective-permute-start.6 = (bf16[6,1,128,128]{2,3,1,0:T(8,128)(2,1)S(1)}, bf16[6,1,128,128]{2,3,1,0:T(8,128)(2,1)}, u32[]{:S(2)}, u32[]{:S(2)}) collective-permute-start(bf16[6,1,128,128]{2,3,1,0:T(8,128)(2,1)S(1)} %get-tuple-element.38), channel_id=1, source_target_pairs={{0,1},{1,2},{2,3},{3,4},{4,5},{5,6},{6,7},{7,8},{8,9},{9,10},{10,1... | collective-permute-start | bytes 589832 | tf_op jit(solution)/shard_map/ppermute | solution.py:16
  105.8 7.8 %copy-start.37 = (s32[1024]{0:T(1024)S(1)}, s32[1024]{0:T(1024)}, u32[]{:S(2)}) copy-start(s32[1024]{0:T(1024)} %copy-done.36) | copy-start | bytes 12292
  106.6 9.2 %copy-start.25 = (f32[4,2]{1,0:T(4,128)S(1)}, f32[4,2]{1,0:T(4,128)}, u32[]{:S(2)}) copy-start(f32[4,2]{1,0:T(4,128)} %copy-done.24) | copy-start | bytes 100
  106.6 9.2 %copy-start.53 = (pred[4,2]{1,0:T(4,128)(4,1)S(1)}, pred[4,2]{1,0:T(4,128)(4,1)}, u32[]{:S(2)}) copy-start(pred[4,2]{1,0:T(4,128)(4,1)} %copy-done.52) | copy-start | bytes 28
  114.9 9.5 %copy-start.7 = (bf16[8,128,128]{1,2,0:T(8,128)(2,1)S(1)}, bf16[8,128,128]{1,2,0:T(8,128)(2,1)}, u32[]{:S(2)}) copy-start(bf16[8,128,128]{1,2,0:T(8,128)(2,1)} %gather_fusion.12) | copy-start | bytes 786436
  115.8 9.5 %copy-start.6 = (bf16[8,128,128]{1,2,0:T(8,128)(2,1)S(1)}, bf16[8,128,128]{1,2,0:T(8,128)(2,1)}, u32[]{:S(2)}) copy-start(bf16[8,128,128]{1,2,0:T(8,128)(2,1)} %gather_fusion.13) | copy-start | bytes 786436
  117.2 8.9 %copy-start.49 = (pred[4,2]{1,0:T(4,128)(4,1)S(1)}, pred[4,2]{1,0:T(4,128)(4,1)}, u32[]{:S(2)}) copy-start(pred[4,2]{1,0:T(4,128)(4,1)} %copy-done.48) | copy-start | bytes 28
  131.5 36.8 %copy-start.41 = (s32[1024]{0:T(1024)S(1)}, s32[1024]{0:T(1024)}, u32[]{:S(2)}) copy-start(s32[1024]{0:T(1024)} %copy-done.40) | copy-start | bytes 12292
  131.5 5.3 %collective-permute-start.9 = (bf16[1,2,128,128]{2,3,1,0:T(8,128)(2,1)S(1)}, bf16[1,2,128,128]{2,3,1,0:T(8,128)(2,1)S(1)}, u32[]{:S(2)}, u32[]{:S(2)}) collective-permute-start(bf16[1,2,128,128]{2,3,1,0:T(8,128)(2,1)S(1)} %get-tuple-element.45), channel_id=1, source_target_pairs={{16,0},{32,16},{48,32},{64,48},{80,64},{96,80},{112,96},{128,112},... | collective-permute-start | bytes 196616 | tf_op jit(solution)/shard_map/ppermute | solution.py:18
  133.5 36.1 %copy-start.31 = (s32[1024]{0:T(1024)S(1)}, s32[1024]{0:T(1024)}, u32[]{:S(2)}) copy-start(s32[1024]{0:T(1024)} %copy-done.30) | copy-start | bytes 12292
  133.5 18.0 %collective-permute-start.8 = (bf16[1,2,128,128]{2,3,1,0:T(8,128)(2,1)S(1)}, bf16[1,2,128,128]{2,3,1,0:T(8,128)(2,1)S(1)}, u32[]{:S(2)}, u32[]{:S(2)}) collective-permute-start(bf16[1,2,128,128]{2,3,1,0:T(8,128)(2,1)S(1)} %get-tuple-element.44), channel_id=1, source_target_pairs={{0,16},{16,32},{32,48},{48,64},{64,80},{80,96},{96,112},{112,128},... | collective-permute-start | bytes 196616 | tf_op jit(solution)/shard_map/ppermute | solution.py:16
  151.5 19.4 %copy-start.29 = (s32[1024]{0:T(1024)S(1)}, s32[1024]{0:T(1024)}, u32[]{:S(2)}) copy-start(s32[1024]{0:T(1024)} %copy-done.28) | copy-start | bytes 12292
  151.5 20.7 %copy-start.35 = (s32[1024]{0:T(1024)S(1)}, s32[1024]{0:T(1024)}, u32[]{:S(2)}) copy-start(s32[1024]{0:T(1024)} %copy-done.34) | copy-start | bytes 12292
  151.6 13.7 %collective-permute-start.11 = (bf16[6,1,128,128]{2,3,1,0:T(8,128)(2,1)S(1)}, bf16[6,1,128,128]{2,3,1,0:T(8,128)(2,1)S(1)}, u32[]{:S(2)}, u32[]{:S(2)}) collective-permute-start(bf16[6,1,128,128]{2,3,1,0:T(8,128)(2,1)S(1)} %get-tuple-element.37), channel_id=1, source_target_pairs={{1,0},{2,1},{3,2},{4,3},{5,4},{6,5},{7,6},{8,7},{9,8},{10,9},{11,1... | collective-permute-start | bytes 589832 | tf_op jit(solution)/shard_map/ppermute | solution.py:18
  163.3 10.2 %copy-start.33 = (s32[1024]{0:T(1024)S(1)}, s32[1024]{0:T(1024)}, u32[]{:S(2)}) copy-start(s32[1024]{0:T(1024)} %copy-done.32) | copy-start | bytes 12292
  163.3 11.4 %copy-start.39 = (s32[1024]{0:T(1024)S(1)}, s32[1024]{0:T(1024)}, u32[]{:S(2)}) copy-start(s32[1024]{0:T(1024)} %copy-done.38) | copy-start | bytes 12292
  163.3 4.9 %collective-permute-start.10 = (bf16[6,1,128,128]{2,3,1,0:T(8,128)(2,1)S(1)}, bf16[6,1,128,128]{2,3,1,0:T(8,128)(2,1)S(1)}, u32[]{:S(2)}, u32[]{:S(2)}) collective-permute-start(bf16[6,1,128,128]{2,3,1,0:T(8,128)(2,1)S(1)} %get-tuple-element.36), channel_id=1, source_target_pairs={{0,1},{1,2},{2,3},{3,4},{4,5},{5,6},{6,7},{7,8},{8,9},{9,10},{10,1... | collective-permute-start | bytes 589832 | tf_op jit(solution)/shard_map/ppermute | solution.py:16
  177.3 10.4 %copy-start.8 = (bf16[8,128,128]{1,2,0:T(8,128)(2,1)S(1)}, bf16[8,128,128]{1,2,0:T(8,128)(2,1)}, u32[]{:S(2)}) copy-start(bf16[8,128,128]{1,2,0:T(8,128)(2,1)} %gather_fusion.19) | copy-start | bytes 786436
  195.0 5.3 %collective-permute-start.13 = (bf16[1,2,128,128]{2,3,1,0:T(8,128)(2,1)S(1)}, bf16[1,2,128,128]{2,3,1,0:T(8,128)(2,1)S(1)}, u32[]{:S(2)}, u32[]{:S(2)}) collective-permute-start(bf16[1,2,128,128]{2,3,1,0:T(8,128)(2,1)S(1)} %get-tuple-element.43), channel_id=1, source_target_pairs={{16,0},{32,16},{48,32},{64,48},{80,64},{96,80},{112,96},{128,112},... | collective-permute-start | bytes 196616 | tf_op jit(solution)/shard_map/ppermute | solution.py:18
  196.9 18.1 %collective-permute-start.12 = (bf16[1,2,128,128]{2,3,1,0:T(8,128)(2,1)S(1)}, bf16[1,2,128,128]{2,3,1,0:T(8,128)(2,1)S(1)}, u32[]{:S(2)}, u32[]{:S(2)}) collective-permute-start(bf16[1,2,128,128]{2,3,1,0:T(8,128)(2,1)S(1)} %get-tuple-element.42), channel_id=1, source_target_pairs={{0,16},{16,32},{32,48},{48,64},{64,80},{80,96},{96,112},{112,128},... | collective-permute-start | bytes 196616 | tf_op jit(solution)/shard_map/ppermute | solution.py:16
  215.1 13.9 %collective-permute-start.15 = (bf16[6,1,128,128]{2,3,1,0:T(8,128)(2,1)S(1)}, bf16[6,1,128,128]{2,3,1,0:T(8,128)(2,1)S(1)}, u32[]{:S(2)}, u32[]{:S(2)}) collective-permute-start(bf16[6,1,128,128]{2,3,1,0:T(8,128)(2,1)S(1)} %get-tuple-element.35), channel_id=1, source_target_pairs={{1,0},{2,1},{3,2},{4,3},{5,4},{6,5},{7,6},{8,7},{9,8},{10,9},{11,1... | collective-permute-start | bytes 589832 | tf_op jit(solution)/shard_map/ppermute | solution.py:18
  226.9 4.9 %collective-permute-start.14 = (bf16[6,1,128,128]{2,3,1,0:T(8,128)(2,1)S(1)}, bf16[6,1,128,128]{2,3,1,0:T(8,128)(2,1)S(1)}, u32[]{:S(2)}, u32[]{:S(2)}) collective-permute-start(bf16[6,1,128,128]{2,3,1,0:T(8,128)(2,1)S(1)} %get-tuple-element.34), channel_id=1, source_target_pairs={{0,1},{1,2},{2,3},{3,4},{4,5},{5,6},{6,7},{7,8},{8,9},{9,10},{10,1... | collective-permute-start | bytes 589832 | tf_op jit(solution)/shard_map/ppermute | solution.py:16
  (24 other events, 50.8 us)
where the time goes:
time: 367 us; the launch traced here: 365 us
  blocking collectives  105 us (29%)
  starting transfers between devices  95.8 us (26%)
  local copies, waits for them, and re-layouts  77.4 us (21%)
  waiting for transfers between devices  58.4 us (16%)
  matrix products  23.2 us (6%)
    psum x1, blocking collectives, on_device(): summed = jnp.stack([lax.psum(term, ('gx', 'gy')) for term in partials])  105 us
    ppermute x8, starting transfers between devices, with_halo(): lax.ppermute(head, axis, [((i + 1) % count, i) for i in range(count)])  75.3 us
    gather x49, local copies, waits for them, and re-layouts, local_apply(): piece = jnp.take(flat, index, axis=0)  65.7 us
    ppermute x8, waiting for transfers between devices, with_halo(): lax.ppermute(tail, axis, [(i, (i + 1) % count) for i in range(count)])  55.2 us
    dot_general x28, matrix products, local_apply(): jnp.einsum('xyrb,xyba->xyra', piece, blocks[:, :, slot], preferred_elemen...  23.2 us
    ppermute x8, starting transfers between devices, with_halo(): lax.ppermute(tail, axis, [(i, (i + 1) % count) for i in range(count)])  20.5 us
  transfers between devices with their start and end apart: 16, of which 9 were waited for; matrix products, arithmetic and copies ran while one was open for 2% of the time, Pallas kernels for 0%

commit v1 on v0

--- a/solution.py
+++ b/solution.py
@@ -61,7 +61,7 @@
         following = 2.0 * image - previous
         previous, current = (current, following)
         partials.append(jnp.sum(first * current, axis=(0, 1, 3)))
-    summed = jnp.stack([lax.psum(term, ("gx", "gy")) for term in partials])
+    summed = jnp.stack([jnp.sum(lax.all_gather(term, ("gx", "gy")), axis=0) for term in partials])
     return (summed / total_rows, current.astype(jnp.bfloat16))
 
 

time: 367 us -> 4310 us (11.74)
  blocking collectives: 105 us -> 4010 us
    all_gather x0 -> x5, blocking collectives: none -> 4010 us  [on_device(): lax.all_gather(term, ('gx', 'gy'))]
    psum x1 -> x0, blocking collectives: 105 us -> none  [on_device(): summed = jnp.stack([lax.psum(term, ('gx', 'gy')) for term in partials])]
  transfers between devices with their start and end apart: 16 -> 16, of which waited for: 9 -> 9; matrix products, arithmetic and copies ran while one was open for 2% -> 0% of each run, Pallas kernels for 0% -> 0%
where the time goes in v1:
time: 4310 us; the launch traced here: 4270 us
  blocking collectives  4010 us (93%)
  starting transfers between devices  96.1 us (2%)
  local copies, waits for them, and re-layouts  77 us (2%)
  waiting for transfers between devices  58.2 us (1%)
    all_gather x5, blocking collectives, on_device(): lax.all_gather(term, ('gx', 'gy'))  4010 us
  transfers between devices with their start and end apart: 16, of which 9 were waited for; matrix products, arithmetic and copies ran while one was open for 0% of the time, Pallas kernels for 0%

profile of v1, /device:TPU:1, one launch (start us, length us, event | category | flops | bytes accessed | tf_op | source)
XLA Modules:
  0.0 4271.9 jit_solution(9306874469861079241)
XLA Ops:
  1.5 4.0 collective-permute-start
  5.6 18.8 collective-permute-start.1
  32.2 4.7 collective-permute-start.3
  36.9 1.9 collective-permute-start.2
  39.2 5.3 collective-permute-done.2
  56.4 12.2 collective-permute-start.5
  68.6 1.9 collective-permute-start.4
  70.5 2.8 collective-permute-done.5
  73.3 13.4 collective-permute-done.4
  87.4 12.2 collective-permute-start.7
  99.6 1.9 collective-permute-start.6
  103.1 1.6 collective-permute-done.6
  106.6 1.4 gather_fusion.8
  108.0 1.4 gather_fusion.9
  109.4 1.4 gather_fusion.10
  110.8 1.4 gather_fusion.11
  112.2 1.4 gather_fusion.12
  117.1 1.8 copy.357
  118.9 1.8 copy.358
  120.7 1.8 copy.359
  122.5 1.8 copy.360
  131.4 1.9 collective-permute-start.9
  133.3 3.4 collective-permute-start.8
  136.7 14.6 collective-permute-done.8
  151.4 11.8 collective-permute-start.11
  163.2 1.9 collective-permute-start.10
  165.1 2.9 collective-permute-done.10
  177.2 1.8 copy.363
  180.3 1.8 copy.364
  182.1 1.8 copy.365
  183.9 1.8 copy.366
  185.7 1.8 copy.367
  194.7 1.9 collective-permute-start.13
  196.7 3.4 collective-permute-start.12
  200.0 14.7 collective-permute-done.12
  214.8 11.8 collective-permute-start.15
  226.6 2.4 collective-permute-start.14
  229.0 2.6 collective-permute-done.14
  240.7 1.8 copy.370
  243.8 1.8 copy.371
  246.4 1.8 copy.373
  248.2 1.8 copy.374
  250.0 1.8 copy.375
  257.8 780.5 %all-gather.5 = f32[512,1,128]{2,1,0:T(1,128)S(1)} all-gather(f32[1,1,128]{2,1,0:T(1,128)S(1)} %bitcast.264), channel_id=2, replica_groups=mesh['gx'=32,'gy'=16] {'gx','gy'}, dimensions={0}, use_global_device_ids=true | all-gather | bytes 262656 | tf_op jit(solution)/shard_map/all_gather | solution.py:64
  1038.3 808.1 %all-gather.6 = f32[512,1,128]{2,1,0:T(1,128)S(1)} all-gather(f32[1,1,128]{2,1,0:T(1,128)S(1)} %bitcast.263), channel_id=3, replica_groups=mesh['gx'=32,'gy'=16] {'gx','gy'}, dimensions={0}, use_global_device_ids=true | all-gather | bytes 262656 | tf_op jit(solution)/shard_map/all_gather | solution.py:64
  1847.5 806.5 %all-gather.7 = f32[512,1,128]{2,1,0:T(1,128)S(1)} all-gather(f32[1,1,128]{2,1,0:T(1,128)S(1)} %bitcast.262), channel_id=4, replica_groups=mesh['gx'=32,'gy'=16] {'gx','gy'}, dimensions={0}, use_global_device_ids=true | all-gather | bytes 262656 | tf_op jit(solution)/shard_map/all_gather | solution.py:64
  2654.5 808.1 %all-gather.8 = f32[512,1,128]{2,1,0:T(1,128)S(1)} all-gather(f32[1,1,128]{2,1,0:T(1,128)S(1)} %bitcast.261), channel_id=5, replica_groups=mesh['gx'=32,'gy'=16] {'gx','gy'}, dimensions={0}, use_global_device_ids=true | all-gather | bytes 262656 | tf_op jit(solution)/shard_map/all_gather | solution.py:64
  3463.2 806.5 %all-gather.9 = f32[512,1,128]{2,1,0:T(1,128)S(1)} all-gather(f32[1,1,128]{2,1,0:T(1,128)S(1)} %bitcast.260), channel_id=6, replica_groups=mesh['gx'=32,'gy'=16] {'gx','gy'}, dimensions={0}, use_global_device_ids=true | all-gather | bytes 262656 | tf_op jit(solution)/shard_map/all_gather | solution.py:64
  (270 shorter events, 74.5 us)
Async XLA Ops:
  1.5 29.6 collective-permute-start
  5.6 26.5 collective-permute-start.1
  28.4 23.2 copy-start.52
  28.4 27.1 copy-start.50
  30.0 22.9 copy-start.48
  30.0 24.3 copy-start.46
  30.1 24.7 copy-start.44
  30.1 25.1 copy-start.42
  30.1 25.9 copy-start.54
  30.9 25.0 copy-start.26
  31.0 14.9 copy-start.30
  31.0 16.2 copy-start.28
  31.0 17.4 copy-start.34
  31.0 18.7 copy-start.32
  31.0 19.3 copy-start.38
  31.0 19.9 copy-start.36
  31.1 14.8 copy-start.40
  32.2 7.1 collective-permute-start.3
  36.9 7.6 collective-permute-start.2
  38.8 12.7 copy-start.24
  38.8 15.9 copy-start.22
  44.6 7.0 copy-start
  55.9 45.6 %copy-start.4 = (bf16[4,2,128,128]{3,2,1,0:T(8,128)(2,1)S(1)}, bf16[4,2,128,128]{3,2,1,0:T(8,128)(2,1)}, u32[]{:S(2)}) copy-start(bf16[4,2,128,128]{3,2,1,0:T(8,128)(2,1)} %param.6) | copy-start | bytes 786436
  56.4 16.9 collective-permute-start.5
  68.6 18.1 collective-permute-start.4
  87.4 15.0 collective-permute-start.7
  99.6 5.1 collective-permute-start.6
  105.8 7.8 copy-start.37
  106.6 9.1 copy-start.25
  106.6 9.1 copy-start.53
  114.9 9.4 copy-start.7
  115.7 9.4 copy-start.6
  117.1 8.9 copy-start.49
  131.4 36.8 copy-start.41
  131.4 5.3 collective-permute-start.9
  133.3 36.1 copy-start.31
  133.3 18.0 collective-permute-start.8
  151.3 19.4 copy-start.29
  151.4 20.7 copy-start.35
  151.4 13.7 collective-permute-start.11
  163.2 10.1 copy-start.33
  163.2 11.4 copy-start.39
  163.2 4.9 collective-permute-start.10
  177.2 10.3 copy-start.8
  194.7 5.3 collective-permute-start.13
  196.7 18.1 collective-permute-start.12
  214.8 14.2 collective-permute-start.15
  226.6 5.0 collective-permute-start.14
  (24 other events, 50.7 us)
